TPU v7x, 32 devices: a whole 2x2x4 slice. The times are simulated.
32 devices in a mesh: batch: 8 (over y, x, core), tensor: 4 (over z).
Axes of the slice: x: 2, y: 2, z: 4, core: 2. Of those that a mesh axis runs over, the one named last changes fastest.
Arguments:
- inputs: bfloat16 [16, 1024, 512], P('batch'), may hold values from -6 to 6
- doc_lengths: int32 [16, 4], P('batch'), may hold values from 1 to 512, 1024 in all within a row
- ln1_gain: float32 [512], replicated, may hold values from 0.5 to 1.5
- ln1_bias: float32 [512], replicated, may hold values from -2.5 to 2.5
- w_qkv: bfloat16 [3, 512, 512], P(None, None, 'tensor'), may hold values from -0.25 to 0.25
- entmax_alpha: float32 [8], P('tensor'), may hold values from 1.15 to 1.5
- w_out: bfloat16 [512, 512], P('tensor'), may hold values from -0.75 to 0.75
- ln2_gain: float32 [512], replicated, may hold values from 0.5 to 1.5
- ln2_bias: float32 [512], replicated, may hold values from -2.5 to 2.5
- w_up: bfloat16 [512, 2048], P(None, 'tensor'), may hold values from -0.25 to 0.25
- up_bias: float32 [2048], P('tensor'), may hold values from -2.5 to 2.5
- w_down: bfloat16 [2048, 512], P('tensor'), may hold values from -0.125 to 0.125
- down_bias: float32 [512], replicated, may hold values from -2.5 to 2.5
- cotangent: bfloat16 [16, 1024, 512], P('batch'), may hold values from -6 to 6
Outputs:
- output: bfloat16 [16, 1024, 512], P('batch')
- grad_input: bfloat16 [16, 1024, 512], P('batch')
- grad_ln1_gain: float32 [512], replicated
- grad_ln1_bias: float32 [512], replicated
- grad_w_qkv: float32 [3, 512, 512], P(None, None, 'tensor')
- grad_alpha: float32 [8], P('tensor')
- grad_w_out: float32 [512, 512], P('tensor')
- grad_ln2_gain: float32 [512], replicated
- grad_ln2_bias: float32 [512], replicated
- grad_w_up: float32 [512, 2048], P(None, 'tensor')
- grad_up_bias: float32 [2048], P('tensor')
- grad_w_down: float32 [2048, 512], P('tensor')
- grad_down_bias: float32 [512], replicated
Inputs may be any that keep to these rules, and one draw needn't show every extreme that they name: `doc_lengths`: each row's 4 lengths sum to 1024, and the largest in each row is 512.
All inputs are finite; a program needn't handle non-finite values.
Results may differ from a plain program's by a relative error of at most 0.03.
Values may be sent and summed in bfloat16 or wider, within the bound.
No kernel may reach another device: no remote copies, remote signals or barrier semaphores. Data moves between devices by JAX's collectives and lax.ppermute only.
A program may use at most 128 MiB of HBM per device.

v0:
```python
import jax
import jax.numpy as jnp
from jax import lax
from jax.sharding import PartitionSpec as P

BISECT = 10


masked_level = -10000.0
tiny_base = 1e-30
norm_eps = 1e-05


def layer_norm(values, norm_gain, norm_shift):
    centre = values - jnp.mean(values, axis=-1, keepdims=True)
    spread = jnp.mean(centre * centre, axis=-1, keepdims=True)
    return centre * lax.rsqrt(spread + norm_eps) * norm_gain + norm_shift


def gelu_tanh(values):
    return jax.nn.gelu(values, approximate=True)


def pow_safe(margin, exponent):
    return jnp.where(margin > 0, jnp.exp(exponent * jnp.log(jnp.maximum(margin, tiny_base))), 0.0)


def entmax_threshold(shifted, allowed, alpha_minus):
    exponent = 1.0 / alpha_minus
    counted = jnp.sum(allowed.astype(shifted.dtype), axis=-1, keepdims=True)
    highest = jnp.max(shifted, axis=-1, keepdims=True)
    low_end = highest - 1.0
    bracket = highest - jnp.exp(-alpha_minus * jnp.log(counted)) - low_end
    for bisect_step in range(BISECT):
        bracket = bracket * 0.5
        middle = low_end + bracket
        summed = jnp.sum(pow_safe(shifted - middle, exponent), axis=-1, keepdims=True)
        low_end = jnp.where(summed >= 1.0, middle, low_end)
    margin = shifted - low_end
    summed = jnp.sum(pow_safe(margin, exponent), axis=-1, keepdims=True)
    slopes = jnp.sum(exponent * pow_safe(margin, exponent - 1.0), axis=-1, keepdims=True)
    return low_end + (summed - 1.0) / slopes


def doc_index(lengths, length):
    doc_ends = jnp.cumsum(lengths)
    places = jnp.arange(length, dtype=jnp.int32)
    return jnp.sum((places[:, None] >= doc_ends[None, :]).astype(jnp.int32), axis=1)


def block_mask(doc_ids, block_start, block_end):
    key_places = jnp.arange(block_end, dtype=jnp.int32)
    row_places = key_places[block_start:block_end]
    return (key_places[None, :] <= row_places[:, None]) & (
        doc_ids[None, :block_end] == doc_ids[block_start:block_end, None]
    )


def block_shifted(query_block, key_rows, allowed, alpha_minus):
    score_scale = query_block.shape[-1] ** (-0.5)
    scores = (
        jnp.einsum("bhe,khe->hbk", query_block, key_rows, preferred_element_type=jnp.float32)
        * score_scale
    )
    return (scores, jnp.where(allowed[None], alpha_minus * scores, masked_level))


def attend_forward(query_rows, key_rows, value_rows, doc_ids, alpha_minus):
    length = query_rows.shape[0]
    block_rows = min(512, length)
    exponent = 1.0 / alpha_minus
    outputs = []
    thresholds = []
    for block_start in range(0, length, block_rows):
        block_end = block_start + block_rows
        allowed = block_mask(doc_ids, block_start, block_end)
        scores, shifted = block_shifted(
            query_rows[block_start:block_end], key_rows[:block_end], allowed, alpha_minus
        )
        threshold = entmax_threshold(shifted, allowed, alpha_minus)
        probs_low = pow_safe(shifted - threshold, exponent).astype(jnp.bfloat16)
        outputs.append(
            jnp.einsum(
                "hbk,khe->bhe",
                probs_low,
                value_rows[:block_end],
                preferred_element_type=jnp.float32,
            )
        )
        thresholds.append(threshold)
    attended = jnp.concatenate(outputs, axis=0)
    return (attended.reshape(length, -1).astype(jnp.bfloat16), jnp.concatenate(thresholds, axis=1))


def attend_backward(query_rows, key_rows, value_rows, doc_ids, thresholds, dattended, alpha_minus):
    length = query_rows.shape[0]
    block_rows = min(512, length)
    score_scale = query_rows.shape[-1] ** (-0.5)
    exponent = 1.0 / alpha_minus
    dkeys = jnp.zeros(key_rows.shape, jnp.float32)
    dvalues = jnp.zeros(value_rows.shape, jnp.float32)
    dalpha = jnp.zeros((alpha_minus.shape[0],), jnp.float32)
    dqueries = []
    for block_start in range(0, length, block_rows):
        block_end = block_start + block_rows
        allowed = block_mask(doc_ids, block_start, block_end)
        query_block = query_rows[block_start:block_end]
        grad_block = dattended[block_start:block_end]
        keys_used = key_rows[:block_end]
        values_used = value_rows[:block_end]
        scores, shifted = block_shifted(query_block, keys_used, allowed, alpha_minus)
        margin = shifted - thresholds[:, block_start:block_end]
        entmax_probs = pow_safe(margin, exponent)
        slopes = exponent * pow_safe(margin, exponent - 1.0)
        dprobs = jnp.einsum(
            "bhe,khe->hbk", grad_block, values_used, preferred_element_type=jnp.float32
        )
        dvalues = dvalues.at[:block_end].add(
            jnp.einsum(
                "hbk,bhe->khe",
                entmax_probs.astype(jnp.bfloat16),
                grad_block,
                preferred_element_type=jnp.float32,
            )
        )
        slope_sum = jnp.sum(slopes, axis=-1, keepdims=True)
        mixed = jnp.sum(slopes * dprobs, axis=-1, keepdims=True)
        centred = dprobs - mixed / slope_sum
        log_margin = jnp.where(margin > 0, jnp.log(jnp.maximum(margin, tiny_base)), 0.0)
        alpha_part = slopes * scores - entmax_probs * log_margin * exponent * exponent
        dalpha = dalpha + jnp.sum(alpha_part * centred, axis=(1, 2))
        dscores = (alpha_minus * (slopes * centred)).astype(jnp.bfloat16)
        dqueries.append(
            jnp.einsum("hbk,khe->bhe", dscores, keys_used, preferred_element_type=jnp.float32)
            * score_scale
        )
        dkeys = dkeys.at[:block_end].add(
            jnp.einsum("hbk,bhe->khe", dscores, query_block, preferred_element_type=jnp.float32)
            * score_scale
        )
    return (jnp.concatenate(dqueries, axis=0), dkeys, dvalues, dalpha)


def shards(
    inputs,
    doc_lengths,
    ln1_gain,
    ln1_bias,
    w_qkv,
    entmax_alpha,
    w_out,
    ln2_gain,
    ln2_bias,
    w_up,
    up_bias,
    w_down,
    down_bias,
    cotangent,
):
    seq_count, length, width = inputs.shape
    heads_here = entmax_alpha.shape[0]
    head_width = w_qkv.shape[2] // heads_here
    alpha_minus = (entmax_alpha - 1.0)[:, None, None]
    token_rows = inputs.reshape(-1, width).astype(jnp.float32)
    normed_one, norm_pull_one = jax.vjp(layer_norm, token_rows, ln1_gain, ln1_bias)
    normed_low = normed_one.astype(jnp.bfloat16)
    projected = jnp.einsum(
        "nd,cde->cne", normed_low, w_qkv, preferred_element_type=jnp.float32
    ).astype(jnp.bfloat16)
    split_heads = projected.reshape(3, seq_count, length, heads_here, head_width)
    doc_ids = jax.vmap(doc_index, (0, None))(doc_lengths, length)

    def forward_sequence(packed):
        return attend_forward(packed[0], packed[1], packed[2], packed[3], alpha_minus)

    attended, thresholds = lax.map(
        forward_sequence, (split_heads[0], split_heads[1], split_heads[2], doc_ids)
    )
    attn_rows = attended.reshape(-1, heads_here * head_width)
    attn_branch = lax.psum(
        jnp.dot(attn_rows, w_out, preferred_element_type=jnp.float32).astype(jnp.bfloat16), "tensor"
    ).astype(jnp.float32)
    resid_here = token_rows + attn_branch
    normed_two, norm_pull_two = jax.vjp(layer_norm, resid_here, ln2_gain, ln2_bias)
    normed_low_two = normed_two.astype(jnp.bfloat16)
    pre_act = jnp.dot(normed_low_two, w_up, preferred_element_type=jnp.float32) + up_bias
    act_full, gelu_pull = jax.vjp(gelu_tanh, pre_act)
    act_low = act_full.astype(jnp.bfloat16)
    ffn_branch = lax.psum(
        jnp.dot(act_low, w_down, preferred_element_type=jnp.float32).astype(jnp.bfloat16), "tensor"
    ).astype(jnp.float32)
    output_low = (resid_here + ffn_branch + down_bias).astype(jnp.bfloat16)
    cot_low = cotangent.reshape(-1, width)
    cot_full = cot_low.astype(jnp.float32)
    grad_w_down = jnp.dot(act_low.T, cot_low, preferred_element_type=jnp.float32)
    grad_down_bias = jnp.sum(cot_full, axis=0)
    dact = jnp.dot(cot_low, w_down.T, preferred_element_type=jnp.float32)
    dpre_low = gelu_pull(dact)[0].astype(jnp.bfloat16)
    grad_w_up = jnp.dot(normed_low_two.T, dpre_low, preferred_element_type=jnp.float32)
    grad_up_bias = jnp.sum(dpre_low.astype(jnp.float32), axis=0)
    dnormed_two = lax.psum(
        jnp.dot(dpre_low, w_up.T, preferred_element_type=jnp.float32).astype(jnp.bfloat16), "tensor"
    ).astype(jnp.float32)
    dresid_part, grad_ln2_gain, grad_ln2_bias = norm_pull_two(dnormed_two)
    dresid = cot_full + dresid_part
    dresid_low = dresid.astype(jnp.bfloat16)
    grad_w_out = jnp.dot(attn_rows.T, dresid_low, preferred_element_type=jnp.float32)
    dattended = jnp.dot(dresid_low, w_out.T, preferred_element_type=jnp.float32).astype(
        jnp.bfloat16
    )
    dattended = dattended.reshape(seq_count, length, heads_here, head_width)

    def backward_sequence(packed):
        return attend_backward(
            packed[0], packed[1], packed[2], packed[3], packed[4], packed[5], alpha_minus
        )

    dquery, dkey, dvalue, dalpha = lax.map(
        backward_sequence,
        (split_heads[0], split_heads[1], split_heads[2], doc_ids, thresholds, dattended),
    )
    grad_alpha = jnp.sum(dalpha, axis=0)
    dqkv_low = (
        jnp.stack([dquery, dkey, dvalue])
        .reshape(3, seq_count * length, heads_here * head_width)
        .astype(jnp.bfloat16)
    )
    grad_w_qkv = jnp.einsum("nd,cne->cde", normed_low, dqkv_low, preferred_element_type=jnp.float32)
    dnormed_one = lax.psum(
        jnp.einsum("cne,cde->nd", dqkv_low, w_qkv, preferred_element_type=jnp.float32).astype(
            jnp.bfloat16
        ),
        "tensor",
    ).astype(jnp.float32)
    dinput_part, grad_ln1_gain, grad_ln1_bias = norm_pull_one(dnormed_one)
    grad_input = (dresid + dinput_part).astype(jnp.bfloat16)
    (
        grad_w_qkv,
        grad_alpha,
        grad_w_out,
        grad_ln1_gain,
        grad_ln1_bias,
        grad_w_up,
        grad_up_bias,
        grad_w_down,
        grad_down_bias,
        grad_ln2_gain,
        grad_ln2_bias,
    ) = lax.psum(
        (
            grad_w_qkv,
            grad_alpha,
            grad_w_out,
            grad_ln1_gain,
            grad_ln1_bias,
            grad_w_up,
            grad_up_bias,
            grad_w_down,
            grad_down_bias,
            grad_ln2_gain,
            grad_ln2_bias,
        ),
        "batch",
    )
    output = output_low.reshape(inputs.shape)
    grad_input = grad_input.reshape(inputs.shape)
    return (
        output,
        grad_input,
        grad_ln1_gain,
        grad_ln1_bias,
        grad_w_qkv,
        grad_alpha,
        grad_w_out,
        grad_ln2_gain,
        grad_ln2_bias,
        grad_w_up,
        grad_up_bias,
        grad_w_down,
        grad_down_bias,
    )


def solution(mesh):
    return jax.shard_map(
        shards,
        mesh=mesh,
        in_specs=(
            P("batch", None, None),
            P("batch", None),
            P(),
            P(),
            P(None, None, "tensor"),
            P("tensor"),
            P("tensor", None),
            P(),
            P(),
            P(None, "tensor"),
            P("tensor"),
            P("tensor", None),
            P(),
            P("batch", None, None),
        ),
        out_specs=(
            P("batch", None, None),
            P("batch", None, None),
            P(),
            P(),
            P(None, None, "tensor"),
            P("tensor"),
            P("tensor", None),
            P(),
            P(),
            P(None, "tensor"),
            P("tensor"),
            P("tensor", None),
            P(),
        ),
        check_vma=False,
    )
```

profile of v0, /device:TPU:0, one launch (start us, length us, event | category | flops | bytes accessed | tf_op | source)
XLA Modules:
  0.0 714.3 jit_solution(8338611175497131669)
XLA Ops:
  17.5 3.2 reshape.2668
  20.7 3.5 copy.76
  24.2 3.2 reshape.2667
  27.4 3.5 copy.75
  32.3 3.5 copy.74
  35.8 102.5 %while.42 = (s32[]{:T(128)}, bf16[2,1024,128]{2,1,0:T(8,128)(2,1)}, f32[2,2,1024,1]{2,1,3,0:T(2,128)S(1)}, bf16[2,1024,2,64]{1,3,2,0:T(8,128)(2,1)}, s32[2,1024]...) while((s32[]{:T(128)}, bf16[2,1024,128]{2,1,0:T(8,128)(2,1)}, ...), condition=%wide.region_33.34_spmd, body=%wide.region_4.33_spmd.sunk | while | flops 534109184 | bytes 87108536 | solution.py:176
  88.0 2.7 select_reduce_fusion.63
  125.9 2.7 select_reduce_fusion.63
  138.3 3.0 convolution_convert_fusion.1
  141.5 89.3 %all-reduce.10.cloned.1.call-done = bf16[2048,512]{1,0:T(8,128)(2,1)} async-done(((bf16[2048,512]{1,0:T(8,128)(2,1)}), bf16[2048,512]{1,0:T(8,128)(2,1)}) %all-reduce.10.cloned.1.call-update) | async-done | bytes 2097168 | tf_op jit(solution)/shard_map/psum | solution.py:180
  237.8 5.3 convert_reduce_fusion.6
  247.2 4.6 fusion.177
  254.1 78.7 %all-reduce.12.cloned.1.call-done = bf16[2048,512]{1,0:T(8,128)(2,1)} async-done(((bf16[2048,512]{1,0:T(8,128)(2,1)}), bf16[2048,512]{1,0:T(8,128)(2,1)}) %all-reduce.12.cloned.1.call-update) | async-done | bytes 2097168 | tf_op jit(solution)/shard_map/psum | solution.py:201
  332.8 5.0 fusion.137
  347.4 71.1 %while.43 = (s32[]{:T(128)}, bf16[2,1024,2,64]{1,3,2,0:T(8,128)(2,1)}, bf16[2,1024,2,64]{1,3,2,0:T(8,128)(2,1)}, bf16[2,1024,2,64]{1,3,2,0:T(8,128)(2,1)}, f32[2...) while((s32[]{:T(128)}, ...), condition=%wide.region_48.49_spmd, body=%wide.region_41.48_spmd.sunk | while | flops 1102247936 | bytes 63729128 | solution.py:218
  354.9 2.6 fusion.269
  362.7 3.2 fusion.274
  365.9 4.3 fusion.263
  370.3 8.0 %fusion.264 = (f32[2]{0:T(128)S(1)}, bf16[2,512,1024]{2,1,0:T(8,128)(2,1)S(1)}) fusion(f32[2,512,1024]{2,1,0:T(8,128)S(1)} %get-tuple-element.972, f32[2,512,1024]{2,1,0:T(8,128)S(1)} %get-tuple-element.976, f32[2,512]{1,0:T(2,128)S(1)} %div.221, f32[2,512]{1,0:T(2,128)S(1)} %get-tuple-element.969, f32[2]{0:T(128)S(1)} %get-tuple-element.970, ...), kind=kLoop, calls=%fused_computation.172.clone.1 | loop fusion | flops 27262974 | bytes 11542568 | tf_op jit(solution)/shard_map/while/body/eval_jaxpr/reduce_sum | solution.py:131
  390.4 2.6 fusion.269
  398.2 3.2 fusion.274
  401.4 4.3 fusion.263
  405.8 8.0 %fusion.264 = (f32[2]{0:T(128)S(1)}, bf16[2,512,1024]{2,1,0:T(8,128)(2,1)S(1)}) fusion(f32[2,512,1024]{2,1,0:T(8,128)S(1)} %get-tuple-element.972, f32[2,512,1024]{2,1,0:T(8,128)S(1)} %get-tuple-element.976, f32[2,512]{1,0:T(2,128)S(1)} %div.221, f32[2,512]{1,0:T(2,128)S(1)} %get-tuple-element.969, f32[2]{0:T(128)S(1)} %get-tuple-element.970, ...), kind=kLoop, calls=%fused_computation.172.clone.1 | loop fusion | flops 27262974 | bytes 11542568 | tf_op jit(solution)/shard_map/while/body/eval_jaxpr/reduce_sum | solution.py:131
  426.7 3.6 copy.100
  430.3 3.1 reshape.2665
  436.2 3.3 fusion.154
  439.5 4.3 convolution_convert_fusion.3
  448.6 60.1 %all-reduce.14.cloned.1.call-done = (f32[3,512,128]{1,2,0:T(8,128)}, f32[128,512]{1,0:T(8,128)}, f32[512,512]{1,0:T(8,128)}, f32[512,512]{1,0:T(8,128)}) async-done(((f32[3,512,128]{1,2,0:T(8,128)}, f32[128,512]{1,0:T(8,128)}, f32[512,512]{1,0:T(8,128)}, f32[512,512]{1,0:T(8,128)}), (f32[3,512,128]{1,2,0:T(8,128)}, f32[128,512]{1,0:T(8,128)}, f32[512,512]{1,0:T(8,128)}, ...) | async-done | bytes 3145744 | tf_op jit(solution)/shard_map/psum | solution.py:249
  510.9 156.1 %all-reduce.16.cloned.1.call-done = (bf16[2048,512]{1,0:T(8,128)(2,1)}, bf16[2048,512]{1,0:T(8,128)(2,1)}) async-done(((bf16[2048,512]{1,0:T(8,128)(2,1)}, bf16[2048,512]{1,0:T(8,128)(2,1)}), (bf16[2048,512]{1,0:T(8,128)(2,1)}, bf16[2048,512]{1,0:T(8,128)(2,1)})) %all-reduce.16.cloned.1.call-update) | async-done | bytes 4194320 | tf_op jit(solution)/shard_map/psum | solution.py:189
  667.1 3.4 convert_reduce_fusion.2
  673.0 24.5 %all-reduce.2 = (f32[512]{0:T(512)}, f32[512]{0:T(512)}, f32[2]{0:T(128)}, f32[512]{0:T(512)}, f32[512]{0:T(512)}, /*index=5*/f32[512]{0:T(512)}, f32[512]{0:T(512)}) all-reduce(f32[512]{0:T(512)S(1)} %get-tuple-element.629, f32[512]{0:T(512)S(1)} %get-tuple-element.632, ...), channel_id=1, replica_groups=mesh['batch'=8,'tensor'=4] {'batch'}, use_global_device_ids=true, to_apply=%region_53.54 | all-reduce | flops 3074 | bytes 24592 | tf_op jit(solution)/shard_map/psum | solution.py:249
  697.6 7.4 %add_convert_fusion = (bf16[2048,512]{1,0:T(8,128)(2,1)}, bf16[2048,512]{1,0:T(8,128)(2,1)}) fusion(bf16[2,1024,512]{2,1,0:T(8,128)(2,1)S(1)} %copy-done.2, bf16[2048,512]{1,0:T(8,128)(2,1)} %get-tuple-element.688, f32[2048,512]{1,0:T(8,128)} %copy-done.5, f32[2048]{0:T(1024)S(1)} %negate_multiply_fusion, f32[2048]{0:T(1024)S(1)} %fusion.159, ...), kind=kLoop, calls=%fused_computation.307 | loop fusion | flops 20971520 | bytes 18919424 | tf_op jit(solution)/shard_map/convert_element_type | solution.py:236
  (330 shorter events, 161.8 us)
Async XLA Ops:
  7.2 229.5 %copy-start = (bf16[512,512]{1,0:T(8,128)(2,1)S(1)}, bf16[512,512]{1,0:T(8,128)(2,1)}, u32[]{:S(2)}) copy-start(bf16[512,512]{1,0:T(8,128)(2,1)} %param.41) | copy-start | bytes 1572868
  7.2 7.0 copy-start.1
  7.2 7.0 copy-start.32
  7.2 7.0 copy-start.37
  7.2 223.5 %all-reduce.10.cloned.1.call-start = ((), (), s32[]{:S(2)}) async-start(), calls=%async_computation | async-start | bytes 4194304 | tf_op jit(solution)/shard_map/psum | solution.py:180
  9.1 6.1 copy-start.41
  35.8 102.5 %copy-start.22 = (bf16[128,512]{1,0:T(8,128)(2,1)S(1)}, bf16[128,512]{1,0:T(8,128)(2,1)}, u32[]{:S(2)}) copy-start(bf16[128,512]{1,0:T(8,128)(2,1)} %param.36) | copy-start | bytes 393220
  141.4 92.8 %copy-start.34 = (f32[512]{0:T(512)S(1)}, f32[512]{0:T(512)}, u32[]{:S(2)}) copy-start(f32[512]{0:T(512)} %param.37) | copy-start | bytes 6148
  141.4 92.8 %copy-start.38 = (f32[512]{0:T(512)S(1)}, f32[512]{0:T(512)}, u32[]{:S(2)}) copy-start(f32[512]{0:T(512)} %param.38) | copy-start | bytes 6148
  141.4 191.3 %all-reduce.12.cloned.1.call-start = ((), (), s32[]{:S(2)}) async-start(), calls=%async_computation.1 | async-start | bytes 4194304 | tf_op jit(solution)/shard_map/psum | solution.py:201
  247.1 261.5 %all-reduce.14.cloned.1.call-start = ((), (), s32[]{:S(2)}) async-start(), calls=%async_computation.2 | async-start | bytes 6291456 | tf_op jit(solution)/shard_map/psum | solution.py:249
  247.2 4.6 copy-start.7
  247.2 4.6 copy-start.44
  332.8 5.0 copy-start.4
  332.8 5.0 copy-start.13
  337.8 4.4 copy-start.8
  422.3 13.8 %copy-start.11 = (bf16[2048,512]{1,0:T(8,128)(2,1)S(1)}, bf16[2048,512]{1,0:T(8,128)(2,1)}, u32[]{:S(2)}) copy-start(bf16[2048,512]{1,0:T(8,128)(2,1)} %copy-done.10) | copy-start | bytes 6291460
  439.5 4.4 copy-start.14
  439.5 227.6 %all-reduce.16.cloned.1.call-start = ((), (), s32[]{:S(2)}) async-start(), calls=%async_computation.3 | async-start | bytes 8388608 | tf_op jit(solution)/shard_map/psum | solution.py:189
  446.4 220.6 %copy-start.2 = (bf16[2,1024,512]{2,1,0:T(8,128)(2,1)S(1)}, bf16[2,1024,512]{2,1,0:T(8,128)(2,1)}, u32[]{:S(2)}) copy-start(bf16[2,1024,512]{2,1,0:T(8,128)(2,1)} %param.30) | copy-start | bytes 6291460
  446.4 220.6 %copy-start.25 = (f32[1,8,2,128]{3,1,2,0:T(8,128)S(1)}, f32[1,8,2,128]{3,1,2,0:T(8,128)}, u32[]{:S(2)}) copy-start(f32[1,8,2,128]{3,1,2,0:T(8,128)} %copy-done.24) | copy-start | bytes 24580
  446.4 220.6 %copy-start.33 = (f32[512]{0:T(512)S(1)}, f32[512]{0:T(512)}, u32[]{:S(2)}) copy-start(f32[512]{0:T(512)} %param.32) | copy-start | bytes 6148
  446.5 224.1 %copy-start.31 = (f32[1,8,2,128]{3,2,1,0:T(2,128)S(1)}, f32[1,8,2,128]{3,2,1,0:T(2,128)}, u32[]{:S(2)}) copy-start(f32[1,8,2,128]{3,2,1,0:T(2,128)} %copy-done.30) | copy-start | bytes 24580
  446.5 224.1 %copy-start.27 = (f32[2048]{0:T(1024)S(1)}, f32[2048]{0:T(1024)}, u32[]{:S(2)}) copy-start(f32[2048]{0:T(1024)} %copy-done.26) | copy-start | bytes 24580
  667.1 5.9 copy-start.35
  667.1 5.9 copy-start.36
  667.1 5.9 copy-start.40
  667.1 30.5 %copy-start.29 = (f32[2048]{0:T(1024)S(1)}, f32[2048]{0:T(1024)}, u32[]{:S(2)}) copy-start(f32[2048]{0:T(1024)} %copy-done.28) | copy-start | bytes 24580
  667.1 30.5 %copy-start.39 = (f32[512]{0:T(512)S(1)}, f32[512]{0:T(512)}, u32[]{:S(2)}) copy-start(f32[512]{0:T(512)} %param.42) | copy-start | bytes 6148
  697.6 7.4 %copy-start.23 = (f32[128,512]{1,0:T(8,128)S(1)}, f32[128,512]{1,0:T(8,128)}, u32[]{:S(2)}) copy-start(f32[128,512]{1,0:T(8,128)} %get-tuple-element.1077) | copy-start | bytes 786436
  697.6 8.1 %copy-start.17 = (f32[512,512]{1,0:T(8,128)S(1)}, f32[512,512]{1,0:T(8,128)}, u32[]{:S(2)}) copy-start(f32[512,512]{1,0:T(8,128)} %get-tuple-element.1080) | copy-start | bytes 3145732
  697.6 9.1 %copy-start.16 = (f32[512,512]{1,0:T(8,128)S(1)}, f32[512,512]{1,0:T(8,128)}, u32[]{:S(2)}) copy-start(f32[512,512]{1,0:T(8,128)} %get-tuple-element.1082) | copy-start | bytes 3145732
  (20 other events, 50.5 us)
Sparse Core Ops, SparseCore 0:
  141.5 89.2 all-reduce.9
  247.2 85.4 all-reduce.11
  439.6 69.0 all-reduce.13
  511.6 155.3 all-reduce.15
where the time goes:
time: 721 us; the launch traced here: 714 us
  waiting for transfers between devices  384 us (53%)
  other arithmetic  117 us (16%)
  matrix products  94.3 us (13%)
  local copies, waits for them, and re-layouts  51.9 us (7%)
  loops' own time  27.7 us (4%)
  blocking collectives  24.5 us (3%)
  between operations  14.6 us (2%)
    psum x1, waiting for transfers between devices, shards(): lax.psum(jnp.dot(act_low, w_down, preferred_element_type=jnp.float32).ast...  156 us
    psum x1, waiting for transfers between devices, shards(): lax.psum(jnp.dot(attn_rows, w_out, preferred_element_type=jnp.float32).as...  89.3 us
    psum x1, waiting for transfers between devices, shards(): lax.psum(jnp.dot(dpre_low, w_up.T, preferred_element_type=jnp.float32).as...  78.7 us
    psum x1, waiting for transfers between devices, shards(): lax.psum((grad_w_qkv, grad_alpha, grad_w_out, grad_ln1_gain, grad_ln1_bia...  60.1 us
    reduce_sum x40, other arithmetic, entmax_threshold(): jnp.sum(pow_safe(shifted - middle, exponent), axis=-1, keepdims=True)  45.9 us
    another operation x1, loops' own time, shards(): lax.map(forward_sequence, (split_heads[0], split_heads[1], split_heads[2]...  27.2 us
    psum x1, blocking collectives, shards(): lax.psum((grad_w_qkv, grad_alpha, grad_w_out, grad_ln1_gain, grad_ln1_bia...  24.5 us
    reduce_sum x4, other arithmetic, attend_backward(): dalpha = dalpha + jnp.sum(alpha_part * centred, axis=(1, 2))  21.3 us
  transfers between devices with their start and end apart: 4, of which 4 were waited for; matrix products, arithmetic and copies ran while one was open for 3% of the time, Pallas kernels for 0%

commit v1 on v0

v1 whole, which is shorter than its diff:
```python
import functools

import jax
import jax.numpy as jnp
from jax import lax
from jax.experimental import pallas as pl
from jax.experimental.pallas import tpu as pltpu
from jax.sharding import PartitionSpec as P

BISECT = 10
MASKED = -10000.0
NORM_EPS = 1e-05
LN2 = 0.6931471805599453
TILE = 128
PLANE = 8
ORDER = (0, 2, 4, 6, 1, 3, 5, 7)
VMEM_BYTES = 48 * 1024 * 1024
BF16 = jnp.bfloat16
F32 = jnp.float32


def layer_norm(values, norm_gain, norm_shift):
    centre = values - jnp.mean(values, axis=-1, keepdims=True)
    spread = jnp.mean(centre * centre, axis=-1, keepdims=True)
    return centre * lax.rsqrt(spread + NORM_EPS) * norm_gain + norm_shift


def gelu_tanh(values):
    return jax.nn.gelu(values, approximate=True)


def dot_nt(left, right):
    return lax.dot_general(left, right, (((1,), (1,)), ((), ())), preferred_element_type=F32)


def dot_nn(left, right):
    return lax.dot_general(left, right, (((1,), (0,)), ((), ())), preferred_element_type=F32)


def dot_tn(left, right):
    return lax.dot_general(left, right, (((0,), (0,)), ((), ())), preferred_element_type=F32)


def tile_mask(first, starts_ref):
    keys = lax.broadcasted_iota(jnp.int32, (first + TILE, TILE), 0)
    queries = lax.broadcasted_iota(jnp.int32, (first + TILE, TILE), 1) + first
    return (keys <= queries) & (keys >= starts_ref[:, first : first + TILE])


def head_lanes(values, head):
    lanes = lax.broadcasted_iota(jnp.int32, values.shape, 1)
    return jnp.where((lanes >= head * 64) & (lanes < head * 64 + 64), values, jnp.zeros_like(values))


def attend_forward(heads, place_ref, alpha_ref, normed_ref, weight_ref, starts_ref,
                   qkv_ref, weight_out_ref, attended_ref, tau_ref, shifted_ref):
    rows = normed_ref.shape[0]
    if len(weight_ref.shape) == 2:
        weight_out_ref[...] = weight_ref[...]
    else:
        part = weight_ref.shape[2]
        for slot, hop in enumerate(ORDER):
            row = pl.multiple_of((place_ref[0] ^ hop) * part, part)
            weight_out_ref[pl.ds(row, part), :] = weight_ref[slot, 0]
    width = heads * 64
    qkv = dot_nn(normed_ref[...], weight_out_ref[...]).astype(BF16)
    qkv_ref[...] = qkv
    queries = qkv[:, :width]
    keys = qkv[:, width : 2 * width]
    values_t = jnp.transpose(qkv[:, 2 * width :].astype(F32)).astype(BF16)
    tiles = [(h, first) for h in range(heads) for first in range(0, rows, TILE)]
    offsets = []
    total = 0
    for h, first in tiles:
        offsets.append(total)
        total += first + TILE
    lows, brackets = [], []
    for (h, first), offset in zip(tiles, offsets):
        alpha_minus = alpha_ref[h] - 1.0
        query = head_lanes(queries[first : first + TILE], h)
        scores = dot_nt(keys[: first + TILE], query) * 0.125
        shifted = jnp.where(tile_mask(first, starts_ref), alpha_minus * scores, MASKED)
        shifted_ref[offset : offset + first + TILE, :] = shifted
        spots = lax.broadcasted_iota(jnp.int32, (1, TILE), 1) + (first + 1)
        counted = (spots - starts_ref[:, first : first + TILE]).astype(F32)
        highest = jnp.max(shifted, axis=0, keepdims=True)
        low = highest - 1.0
        lows.append(low)
        brackets.append(highest - jnp.exp(-alpha_minus * jnp.log(counted)) - low)

    def bisect(step, carry):
        lows, brackets = carry
        new_lows, new_brackets = [], []
        for (h, first), offset, low, bracket in zip(tiles, offsets, lows, brackets):
            bracket = bracket * 0.5
            middle = low + bracket
            power = 1.0 / ((alpha_ref[h] - 1.0) * LN2)
            margin = jnp.maximum(shifted_ref[offset : offset + first + TILE, :] - middle, 0.0)
            summed = jnp.sum(jnp.exp2(power * jnp.log(margin)), axis=0, keepdims=True)
            new_lows.append(jnp.where(summed >= 1.0, middle, low))
            new_brackets.append(bracket)
        return tuple(new_lows), tuple(new_brackets)

    lows, _ = lax.fori_loop(0, BISECT, bisect, (tuple(lows), tuple(brackets)))
    for (h, first), offset, low in zip(tiles, offsets, lows):
        exponent = 1.0 / (alpha_ref[h] - 1.0)
        shifted = shifted_ref[offset : offset + first + TILE, :]
        margin = jnp.maximum(shifted - low, 0.0)
        slope = jnp.exp2((exponent - 1.0) * (1.0 / LN2) * jnp.log(margin))
        slopes = exponent * jnp.sum(slope, axis=0, keepdims=True)
        summed = jnp.sum(slope * margin, axis=0, keepdims=True)
        tau = low + (summed - 1.0) / slopes
        tau_ref[h : h + 1, first : first + TILE] = tau
        margin = jnp.maximum(shifted - tau, 0.0)
        probs = jnp.exp2(exponent * (1.0 / LN2) * jnp.log(margin)).astype(BF16)
        out = dot_nn(values_t[h * 64 : h * 64 + 64, : first + TILE], probs)
        attended_ref[first : first + TILE, h * 64 : h * 64 + 64] = jnp.transpose(out).astype(BF16)


def attend_backward(heads, place_ref, alpha_ref, normed_ref, qkv_ref, tau_ref, starts_ref, dattended_ref,
                    dqkv_ref, grad_ref, dalpha_ref, dkeys_ref, dvalues_ref):
    rows = normed_ref.shape[0]
    width = heads * 64
    queries = qkv_ref[:, :width]
    keys = qkv_ref[:, width : 2 * width]
    values = qkv_ref[:, 2 * width :]
    keys_t = jnp.transpose(keys.astype(F32)).astype(BF16)
    dkeys_ref[...] = jnp.zeros_like(dkeys_ref)
    dvalues_ref[...] = jnp.zeros_like(dvalues_ref)
    for h in range(heads):
        alpha_minus = alpha_ref[h] - 1.0
        exponent = 1.0 / alpha_minus
        dalpha = jnp.zeros((1, TILE), F32)
        for first in range(0, rows, TILE):
            end = first + TILE
            query = head_lanes(queries[first:end], h)
            dout = head_lanes(dattended_ref[first:end, :], h)
            scores = dot_nt(keys[:end], query) * 0.125
            shifted = jnp.where(tile_mask(first, starts_ref), alpha_minus * scores, MASKED)
            margin = jnp.maximum(shifted - tau_ref[h : h + 1, first:end], 0.0)
            log_margin = jnp.log(margin)
            slope = jnp.exp2((exponent - 1.0) * (1.0 / LN2) * log_margin)
            probs = slope * margin
            slope = exponent * slope
            dprobs = dot_nt(values[:end], dout)
            slope_sum = jnp.sum(slope, axis=0, keepdims=True)
            mixed = jnp.sum(slope * dprobs, axis=0, keepdims=True)
            centred = dprobs - mixed / slope_sum
            log_margin = jnp.where(margin > 0.0, log_margin, 0.0)
            alpha_part = slope * scores - (exponent * exponent) * (probs * log_margin)
            dalpha = dalpha + jnp.sum(alpha_part * centred, axis=0, keepdims=True)
            dscores = (alpha_minus * (slope * centred)).astype(BF16)
            dvalues_ref[:end, :] += dot_nn(probs.astype(BF16), dout)
            dkeys_ref[:end, :] += dot_nn(dscores, query)
            dquery_t = dot_nn(keys_t[h * 64 : h * 64 + 64, :end], dscores) * 0.125
            dqkv_ref[first:end, h * 64 : h * 64 + 64] = jnp.transpose(dquery_t).astype(BF16)
        dalpha_ref[h : h + 1, :] = dalpha
    dqkv_ref[:, width : 2 * width] = (dkeys_ref[...] * 0.125).astype(BF16)
    dqkv_ref[:, 2 * width :] = dvalues_ref[...].astype(BF16)
    grad = dot_tn(normed_ref[...], dqkv_ref[...]).astype(BF16)
    part = grad_ref.shape[1]
    for spot in range(PLANE):
        hop = place_ref[0] ^ spot
        grad_ref[(hop % 2) * 4 + hop // 2] = grad[spot * part : (spot + 1) * part]


def whole(shape):
    return pl.BlockSpec(shape, lambda *_: (0,) * len(shape), memory_space=pltpu.VMEM)


def run_forward(heads, place, alpha, normed, weight, slot, starts):
    rows, width = normed.shape
    columns = 3 * heads * 64
    total = heads * sum(range(TILE, rows + 1, TILE))
    if slot == 0:
        weight_spec = whole(weight.shape)
    else:
        block = (weight.shape[0], 1) + weight.shape[2:]
        weight_spec = pl.BlockSpec(block, lambda _: (0, slot - 1, 0, 0), memory_space=pltpu.VMEM)
    smem = pl.BlockSpec(memory_space=pltpu.SMEM)
    return pl.pallas_call(
        functools.partial(attend_forward, heads),
        out_shape=(
            jax.ShapeDtypeStruct((rows, columns), BF16),
            jax.ShapeDtypeStruct((width, columns), BF16),
            jax.ShapeDtypeStruct((rows, heads * 64), BF16),
            jax.ShapeDtypeStruct((heads, rows), F32),
        ),
        grid=(1,),
        in_specs=[smem, smem, whole(normed.shape), weight_spec, whole(starts.shape)],
        out_specs=(
            whole((rows, columns)),
            whole((width, columns)),
            whole((rows, heads * 64)),
            whole((heads, rows)),
        ),
        scratch_shapes=[pltpu.VMEM((total, TILE), F32)],
        compiler_params=pltpu.CompilerParams(vmem_limit_bytes=VMEM_BYTES),
        cost_estimate=pl.CostEstimate(flops=3 * 10**9, bytes_accessed=2 * 10**6, transcendentals=10**7),
        name="attend_forward",
    )(place, alpha, normed, weight, starts)


def run_backward(heads, place, alpha, normed, qkv, tau, starts, dattended):
    rows, width = normed.shape
    columns = 3 * heads * 64
    smem = pl.BlockSpec(memory_space=pltpu.SMEM)
    return pl.pallas_call(
        functools.partial(attend_backward, heads),
        out_shape=(
            jax.ShapeDtypeStruct((rows, columns), BF16),
            jax.ShapeDtypeStruct((PLANE, width // PLANE, columns), BF16),
            jax.ShapeDtypeStruct((heads, TILE), F32),
        ),
        grid=(1,),
        in_specs=[smem, smem] + [whole(a.shape) for a in (normed, qkv, tau, starts, dattended)],
        out_specs=(
            whole((rows, columns)),
            whole((PLANE, width // PLANE, columns)),
            whole((heads, TILE)),
        ),
        scratch_shapes=[pltpu.VMEM((rows, heads * 64), F32), pltpu.VMEM((rows, heads * 64), F32)],
        compiler_params=pltpu.CompilerParams(vmem_limit_bytes=VMEM_BYTES),
        cost_estimate=pl.CostEstimate(flops=3 * 10**9, bytes_accessed=2 * 10**6, transcendentals=10**7),
        name="attend_backward",
    )(place, alpha, normed, qkv, tau, starts, dattended)


def solution(mesh):
    batch_size = mesh.shape["batch"]
    tensor_size = mesh.shape["tensor"]

    def over_batch(array, hop):
        return lax.ppermute(array, "batch", [(i, i ^ hop) for i in range(batch_size)])

    def over_tensor(array, hop):
        return lax.ppermute(array, "tensor", [(i, i ^ hop) for i in range(tensor_size)])

    def gather_plane(array):
        across = jnp.stack([array] + [over_batch(array, hop) for hop in (2, 4, 6)])
        return jnp.concatenate([across, over_batch(across, 1)])

    def gather_weight(part):
        received = jnp.stack([over_tensor(part, hop) for hop in range(1, tensor_size)])
        return gather_plane(received)

    def reduce_all(grads):
        half = (grads[:, :4].astype(F32) + over_batch(grads[:, 4:], 1).astype(F32)).astype(BF16)
        across = [over_batch(half[:, hop // 2], hop).astype(F32) for hop in (2, 4, 6)]
        quarter = (half[:, 0].astype(F32) + across[0]) + (across[1] + across[2])
        hop = PLANE
        while hop < batch_size:
            quarter = quarter + over_batch(quarter.astype(BF16), hop).astype(F32)
            hop *= 2
        quarter = quarter.astype(BF16)
        lines = [over_tensor(quarter[hop], hop).astype(F32) for hop in range(1, tensor_size)]
        return (quarter[0].astype(F32) + lines[0]) + (lines[1] + lines[2])

    def sum_small(array):
        hops = [array] + [over_batch(array, hop) for hop in range(1, PLANE)]
        array = ((hops[0] + hops[1]) + (hops[2] + hops[3])) + ((hops[4] + hops[5]) + (hops[6] + hops[7]))
        hop = PLANE
        while hop < batch_size:
            array = array + over_batch(array, hop)
            hop *= 2
        return array

    def shards(inputs, doc_lengths, ln1_gain, ln1_bias, w_qkv, entmax_alpha, w_out, ln2_gain, ln2_bias,
               w_up, up_bias, w_down, down_bias, cotangent):
        seq_count, length, width = inputs.shape
        heads = entmax_alpha.shape[0]
        hidden = w_up.shape[1]
        rows = length // 2
        columns = heads * 64
        place = lax.axis_index("batch") % PLANE
        line = lax.axis_index("tensor")
        hops = [place ^ hop for hop in ORDER]

        ends = jnp.cumsum(doc_lengths, axis=1)
        firsts = ends - doc_lengths
        big = jnp.sum(jnp.where(doc_lengths == rows, firsts, 0), axis=1)

        def unit_start(unit):
            return (jnp.take(big, unit // 2) + rows * (unit % 2)) % length

        start = unit_start(line)
        doc_places = (jnp.take(firsts, line // 2, axis=0) - start) % length
        spots = jnp.arange(rows, dtype=jnp.int32)
        starts = jnp.max(
            jnp.where(doc_places[:, None] <= spots[None, :], doc_places[:, None], 0), axis=0, keepdims=True
        )

        def own_rows(array):
            one = lax.dynamic_index_in_dim(array, line // 2, 0, keepdims=False)
            return lax.dynamic_slice_in_dim(jnp.concatenate([one, one[:rows]]), start, rows)

        def relative(array):
            parts = array.reshape((PLANE, array.shape[0] // PLANE) + array.shape[1:])
            return jnp.concatenate([lax.dynamic_index_in_dim(parts, hop, 0, keepdims=False) for hop in hops])

        def own_part(array):
            return lax.dynamic_slice_in_dim(array, place * (array.shape[0] // PLANE), array.shape[0] // PLANE)

        def natural(parts):
            spots = [(spot ^ place) for spot in range(PLANE)]
            return jnp.concatenate(
                [
                    lax.dynamic_index_in_dim(parts, (spot % 2) * 4 + spot // 2, 0, keepdims=False)
                    for spot in spots
                ]
            )

        qkv_own = jnp.transpose(w_qkv, (1, 0, 2)).reshape(width, 3 * columns)
        up_own = jnp.transpose(w_up)
        qkv_far = gather_weight(own_part(qkv_own))
        rest_far = gather_weight(jnp.concatenate([own_part(w_out), own_part(up_own), own_part(w_down)]))
        small = jnp.concatenate([up_bias, entmax_alpha])
        small_far = [over_tensor(small, hop) for hop in range(1, tensor_size)]
        alphas = [entmax_alpha] + [far[hidden:] for far in small_far]
        out_part = w_out.shape[0] // PLANE
        up_part = hidden // PLANE

        tokens = own_rows(inputs).astype(F32)
        cot_low = own_rows(cotangent)
        normed_one, pull_one = jax.vjp(layer_norm, tokens, ln1_gain, ln1_bias)
        normed_low = normed_one.astype(BF16)
        place_ref = place.reshape(1)

        qkvs, weights, attendeds, taus = [], [], [], []
        for slot in range(tensor_size):
            qkv, weight, attended, tau = run_forward(
                heads, place_ref, alphas[slot], normed_low, qkv_own if slot == 0 else qkv_far, slot, starts
            )
            qkvs.append(qkv)
            weights.append(weight)
            attendeds.append(attended)
            taus.append(tau)

        out_weights = jnp.concatenate(
            [w_out] + [natural(rest_far[:, hop, :out_part]) for hop in range(tensor_size - 1)]
        )
        up_weights = jnp.concatenate(
            [relative(up_own)]
            + [
                rest_far[:, hop, out_part : out_part + up_part].reshape(hidden, width)
                for hop in range(tensor_size - 1)
            ]
        )
        down_weights = jnp.concatenate(
            [relative(w_down)]
            + [rest_far[:, hop, out_part + up_part :].reshape(hidden, width) for hop in range(tensor_size - 1)]
        )
        up_biases = jnp.concatenate([relative(up_bias)] + [relative(far[:hidden]) for far in small_far])
        attended = jnp.concatenate(attendeds, axis=1)

        resid = tokens + dot_nn(attended, out_weights)
        normed_two, pull_two = jax.vjp(layer_norm, resid, ln2_gain, ln2_bias)
        normed_low_two = normed_two.astype(BF16)
        pre_act = dot_nt(normed_low_two, up_weights) + up_biases
        act, pull_gelu = jax.vjp(gelu_tanh, pre_act)
        act_low = act.astype(BF16)
        out_low = (resid + dot_nn(act_low, down_weights) + down_bias).astype(BF16)

        def gather_units(chunk):
            far = [chunk] + [over_tensor(chunk, hop) for hop in range(1, tensor_size)]
            here = jnp.concatenate(far[:2])
            there = jnp.concatenate(far[2:])
            here = jnp.roll(here, start, axis=0)
            there = jnp.roll(there, unit_start(line ^ 2), axis=0)
            first = line // 2 == 0
            return jnp.stack([jnp.where(first, here, there), jnp.where(first, there, here)])

        output = gather_units(out_low)

        grad_down = dot_tn(act_low, cot_low).astype(BF16)
        cot_full = cot_low.astype(F32)
        dact = dot_nt(cot_low, down_weights)
        dpre = pull_gelu(dact)[0].astype(BF16)
        grad_up = dot_tn(dpre, normed_low_two).astype(BF16)
        dnormed_two = dot_nn(dpre, up_weights)
        dresid_part, grad_ln2_gain, grad_ln2_bias = pull_two(dnormed_two)
        dresid = cot_full + dresid_part
        dresid_low = dresid.astype(BF16)
        dattended = dot_nt(dresid_low, out_weights).astype(BF16)
        grad_out = dot_tn(attended, dresid_low).astype(BF16)

        grad_qkv, dqkvs, dalphas = [], [], []
        for slot in range(tensor_size):
            dqkv, grad, dalpha = run_backward(
                heads, place_ref, alphas[slot], normed_low, qkvs[slot], taus[slot], starts,
                dattended[:, slot * columns : (slot + 1) * columns],
            )
            dqkvs.append(dqkv)
            grad_qkv.append(grad)
            dalphas.append(jnp.sum(dalpha, axis=1))
        dnormed_one = dot_nt(jnp.concatenate(dqkvs, axis=1), jnp.concatenate(weights, axis=1))
        dinput_part, grad_ln1_gain, grad_ln1_bias = pull_one(dnormed_one)
        grad_input = gather_units((dresid + dinput_part).astype(BF16))

        def by_part(array):
            return array.reshape(tensor_size, PLANE, array.shape[0] // (tensor_size * PLANE), array.shape[1])

        grad_ffn = jnp.concatenate([by_part(grad_up), by_part(grad_down)], axis=2)
        ffn_sum = gather_plane(reduce_all(grad_ffn).astype(BF16))
        qkv_sum = gather_plane(reduce_all(jnp.stack(grad_qkv)).astype(BF16))
        out_parts = by_part(grad_out)
        out_parts = jnp.stack([relative(out_parts[slot]) for slot in range(tensor_size)])
        out_sum = gather_plane(reduce_all(out_parts).astype(BF16))
        grad_w_up = jnp.transpose(natural(ffn_sum[:, :up_part]).astype(F32))
        grad_w_down = natural(ffn_sum[:, up_part:]).astype(F32)
        grad_w_qkv = jnp.transpose(natural(qkv_sum).astype(F32).reshape(width, 3, columns), (1, 0, 2))
        grad_w_out = natural(out_sum).astype(F32)

        grad_bias = jnp.sum(dpre.astype(F32), axis=0).reshape(tensor_size, PLANE, up_part)
        grad_bias = jnp.stack([natural(grad_bias[slot]) for slot in range(tensor_size)])
        common = jnp.concatenate(
            [grad_ln1_gain, grad_ln1_bias, grad_ln2_gain, grad_ln2_bias, jnp.sum(cot_full, axis=0)]
        )
        lines = jnp.concatenate([grad_bias, jnp.stack(dalphas)], axis=1)
        small_sum = sum_small(jnp.concatenate([common, lines.reshape(-1)]))
        common = small_sum[: 5 * width]
        lines = small_sum[5 * width :].reshape(tensor_size, hidden + heads)
        commons = [common] + [over_tensor(common, hop) for hop in range(1, tensor_size)]
        common = ((commons[0] + commons[1]) + (commons[2] + commons[3])).reshape(5, width)
        own = [lines[0]] + [over_tensor(lines[hop], hop) for hop in range(1, tensor_size)]
        own = (own[0] + own[1]) + (own[2] + own[3])
        return (
            output,
            grad_input,
            common[0],
            common[1],
            grad_w_qkv,
            own[hidden:],
            grad_w_out,
            common[2],
            common[3],
            grad_w_up,
            own[:hidden],
            grad_w_down,
            common[4],
        )

    return jax.shard_map(
        shards,
        mesh=mesh,
        in_specs=(
            P("batch", None, None),
            P("batch", None),
            P(),
            P(),
            P(None, None, "tensor"),
            P("tensor"),
            P("tensor", None),
            P(),
            P(),
            P(None, "tensor"),
            P("tensor"),
            P("tensor", None),
            P(),
            P("batch", None, None),
        ),
        out_specs=(
            P("batch", None, None),
            P("batch", None, None),
            P(),
            P(),
            P(None, None, "tensor"),
            P("tensor"),
            P("tensor", None),
            P(),
            P(),
            P(None, "tensor"),
            P("tensor"),
            P("tensor", None),
            P(),
        ),
        check_vma=False,
    )
```

time: 721 us -> 379 us (0.53)
  waiting for transfers between devices: 384 us -> 145 us
  starting transfers between devices: 0.16 us -> 78 us
  other arithmetic: 117 us -> 42.3 us
  matrix products: 94.3 us -> 23 us
  Pallas kernels: 0 us -> 43.1 us
  loops' own time: 27.7 us -> 0 us
  blocking collectives: 24.5 us -> 0 us
  local copies, waits for them, and re-layouts: 51.9 us -> 38.5 us
  between operations: 14.6 us -> 4.69 us
    psum x4 -> x0, waiting for transfers between devices: 384 us -> none  [the longest x1 156 us: shards(): lax.psum(jnp.dot(act_low, w_down, preferred_element_type=jnp.float32).ast...]
    ppermute x0 -> x69, waiting for transfers between devices: none -> 145 us  [the longest x30 84.9 us: over_tensor(): lax.ppermute(array, 'tensor', [(i, i ^ hop) for i in range(tensor_size)])]
    reduce_sum x58 -> x7, other arithmetic: 89.4 us -> 5.04 us  [the longest x1 1.79 us: layer_norm(): return centre * lax.rsqrt(spread + NORM_EPS) * norm_gain + norm_shift]
    ppermute x0 -> x69, starting transfers between devices: none -> 78 us  [the longest x30 39.6 us: over_tensor(): lax.ppermute(array, 'tensor', [(i, i ^ hop) for i in range(tensor_size)])]
    dot_general x40 -> x10, matrix products: 94.3 us -> 23 us  [the longest x4 8.02 us: dot_nt(): lax.dot_general(left, right, (((1,), (1,)), ((), ())), preferred_element_...]
    pallas_call x0 -> x8, Pallas kernels: none -> 43.1 us  [the longest x4 26.6 us: run_forward(): pl.pallas_call(functools.partial(attend_forward, heads), out_shape=(jax.S...]
    another operation x2 -> x0, loops' own time: 27.7 us -> none  [the longest x1 27.2 us: shards(): lax.map(forward_sequence, (split_heads[0], split_heads[1], split_heads[2]...]
    another operation x5 -> x16, other arithmetic: 1.01 us -> 26.5 us  [the longest x6 25.5 us: gather_units(): jnp.stack([jnp.where(first, here, there), jnp.where(first, there, here)])]
  transfers between devices with their start and end apart: 4 -> 69, of which waited for: 4 -> 35; matrix products, arithmetic and copies ran while one was open for 3% -> 16% of each run, Pallas kernels for 0% -> 7%
where the time goes in v1:
time: 379 us; the launch traced here: 375 us
  waiting for transfers between devices  145 us (38%)
  starting transfers between devices  78 us (21%)
  Pallas kernels  43.1 us (11%)
  other arithmetic  42.3 us (11%)
  local copies, waits for them, and re-layouts  38.5 us (10%)
  matrix products  23 us (6%)
  between operations  4.69 us (1%)
    ppermute x30, waiting for transfers between devices, over_tensor(): lax.ppermute(array, 'tensor', [(i, i ^ hop) for i in range(tensor_size)])  84.9 us
    ppermute x39, waiting for transfers between devices, over_batch(): lax.ppermute(array, 'batch', [(i, i ^ hop) for i in range(batch_size)])  60.3 us
    ppermute x30, starting transfers between devices, over_tensor(): lax.ppermute(array, 'tensor', [(i, i ^ hop) for i in range(tensor_size)])  39.6 us
    ppermute x39, starting transfers between devices, over_batch(): lax.ppermute(array, 'batch', [(i, i ^ hop) for i in range(batch_size)])  38.4 us
    pallas_call x4, Pallas kernels, run_forward(): pl.pallas_call(functools.partial(attend_forward, heads), out_shape=(jax.S...  26.6 us
    another operation x6, other arithmetic, gather_units(): jnp.stack([jnp.where(first, here, there), jnp.where(first, there, here)])  25.5 us
    unnamed x249, local copies, waits for them, and re-layouts  24.1 us
    pallas_call x4, Pallas kernels, run_backward(): pl.pallas_call(functools.partial(attend_backward, heads), out_shape=(jax....  16.6 us
  transfers between devices with their start and end apart: 69, of which 35 were waited for; matrix products, arithmetic and copies ran while one was open for 16% of the time, Pallas kernels for 7%

profile of v1, /device:TPU:0, one launch (start us, length us, event | category | flops | bytes accessed | tf_op | source)
XLA Modules:
  0.0 374.8 jit_solution(15329380593492602602)
XLA Ops:
  2.1 5.0 %collective-permute-start.9 = (f32[514]{0:T(1024)S(1)}, f32[514]{0:T(1024)S(1)}, u32[]{:S(2)}, u32[]{:S(2)}) collective-permute-start(f32[514]{0:T(1024)S(1)} %constant_dynamic-update-slice_fusion.134), channel_id=1, source_target_pairs={{0,3},{1,2},{2,1},{3,0},{4,7},{5,6},{6,5},{7,4},{8,11},{9,10},{10,... | collective-permute-start | bytes 6176 | tf_op jit(solution)/shard_map/ppermute | solution.py:237
  9.1 3.9 %collective-permute-start.3 = (bf16[64,384]{1,0:T(8,128)(2,1)S(1)}, bf16[64,384]{1,0:T(8,128)(2,1)S(1)}, u32[]{:S(2)}, u32[]{:S(2)}) collective-permute-start(bf16[64,384]{1,0:T(8,128)(2,1)S(1)} %constant_dynamic-slice_fusion.147), channel_id=1, source_target_pairs={{0,3},{1,2},{2,1},{3,0},{4,7},{5,6},{6,5},{7,4},{8,11},{9,10},{10,... | collective-permute-start | bytes 147464 | tf_op jit(solution)/shard_map/ppermute | solution.py:237
  16.7 2.7 dynamic-slice_bitcast_fusion
  23.4 6.7 %attend_forward.4 = (bf16[512,384]{1,0:T(8,128)(2,1)S(1)}, bf16[512,384]{1,0:T(8,128)(2,1)S(1)}, bf16[512,128]{1,0:T(8,128)(2,1)S(1)}, f32[2,512]{1,0:T(2,128)S(1)}) custom-call(s32[1]{0:T(128)} %bitcast.3.place_ref, f32[2]{0:T(128)S(1)} %copy-done, bf16[512,512]{1,0:T(8,128)(2,1)S(1)} %fusion.32.normed_ref, bf16[512,384]{1,0:T(8,128)(2,1)S(1)} %copy.74.weight_ref, ...), custom_call_target="tpu_custom_call" | custom-call | flops 3000000000 | bytes 2000000 | tf_op jit(solution)/shard_map/attend_forward/pallas_call | solution.py:181
  43.0 3.7 collective-permute-start.12
  54.9 2.6 collective-permute-done.11
  61.5 8.3 %collective-permute-done.14 = bf16[3,144,512]{2,1,0:T(8,128)(2,1)S(1)} collective-permute-done((bf16[3,144,512]{2,1,0:T(8,128)(2,1)S(1)}, bf16[3,144,512]{2,1,0:T(8,128)(2,1)S(1)}, u32[]{:S(2)}, u32[]{:S(2)}) %collective-permute-start.14) | collective-permute-done | bytes 442400 | tf_op jit(solution)/shard_map/ppermute | solution.py:234
  72.3 6.7 %collective-permute-done.15 = bf16[3,144,512]{2,1,0:T(8,128)(2,1)S(1)} collective-permute-done((bf16[3,144,512]{2,1,0:T(8,128)(2,1)S(1)}, bf16[3,144,512]{2,1,0:T(8,128)(2,1)S(1)}, u32[]{:S(2)}, u32[]{:S(2)}) %collective-permute-start.15) | collective-permute-done | bytes 442400 | tf_op jit(solution)/shard_map/ppermute | solution.py:234
  79.5 6.6 %attend_forward.5 = (bf16[512,384]{1,0:T(8,128)(2,1)S(1)}, bf16[512,384]{1,0:T(8,128)(2,1)S(1)}, bf16[512,128]{1,0:T(8,128)(2,1)S(1)}, f32[2,512]{1,0:T(2,128)S(1)}) custom-call(s32[1]{0:T(128)} %bitcast.3.place_ref, f32[2]{0:T(128)S(1)} %slice.281.alpha_ref, bf16[512,512]{1,0:T(8,128)(2,1)S(1)} %fusion.32.normed_ref, ...), custom_call_target="tpu_custom_call" | custom-call | flops 3000000000 | bytes 2000000 | tf_op jit(solution)/shard_map/attend_forward/pallas_call | solution.py:181
  86.2 6.6 %attend_forward.6 = (bf16[512,384]{1,0:T(8,128)(2,1)S(1)}, bf16[512,384]{1,0:T(8,128)(2,1)S(1)}, bf16[512,128]{1,0:T(8,128)(2,1)S(1)}, f32[2,512]{1,0:T(2,128)S(1)}) custom-call(s32[1]{0:T(128)} %bitcast.3.place_ref, f32[2]{0:T(128)S(1)} %slice.282.alpha_ref, bf16[512,512]{1,0:T(8,128)(2,1)S(1)} %fusion.32.normed_ref, ...), custom_call_target="tpu_custom_call" | custom-call | flops 3000000000 | bytes 2000000 | tf_op jit(solution)/shard_map/attend_forward/pallas_call | solution.py:181
  92.8 6.8 %attend_forward.7 = (bf16[512,384]{1,0:T(8,128)(2,1)S(1)}, bf16[512,384]{1,0:T(8,128)(2,1)S(1)}, bf16[512,128]{1,0:T(8,128)(2,1)S(1)}, f32[2,512]{1,0:T(2,128)S(1)}) custom-call(s32[1]{0:T(128)} %bitcast.3.place_ref, f32[2]{0:T(128)S(1)} %slice.283.alpha_ref, bf16[512,512]{1,0:T(8,128)(2,1)S(1)} %fusion.32.normed_ref, ...), custom_call_target="tpu_custom_call" | custom-call | flops 3000000000 | bytes 2000000 | tf_op jit(solution)/shard_map/attend_forward/pallas_call | solution.py:181
  106.2 3.5 convolution_convert_fusion
  109.7 4.2 %convert_reduce_fusion = (f32[2048]{0:T(1024)S(1)}, bf16[512,2048]{1,0:T(8,128)(2,1)S(1)}) fusion(f32[512,2048]{1,0:T(8,128)S(1)} %fusion.201, f32[2048]{0:T(1024)S(1)} %concatenate.138, bf16[512,512]{1,0:T(8,128)(2,1)S(1)} %copy-done.23, bf16[2048,512]{1,0:T(8,128)(2,1)S(1)} %constant_dynamic-update-slice_fusion.51), kind=kOutput, calls=%fused_computation.12 | convolution fusion | flops 1097857024 | bytes 8929280 | tf_op jit(solution)/shard_map/dot_general | solution.py:33
  116.0 2.8 convolution_convert_fusion.1
  122.9 4.1 %attend_backward.4 = (bf16[512,384]{1,0:T(8,128)(2,1)S(1)}, bf16[8,64,384]{2,1,0:T(8,128)(2,1)S(1)}, f32[2,128]{1,0:T(2,128)S(1)}) custom-call(s32[1]{0:T(128)} %bitcast.3.place_ref, f32[2]{0:T(128)S(1)} %copy-done, bf16[512,512]{1,0:T(8,128)(2,1)S(1)} %fusion.32.normed_ref, bf16[512,384]{1,0:T(8,128)(2,1)S(1)} %get-tuple-element.46.qkv_ref, ...), custom_call_target="tpu_custom_call" | custom-call | flops 3000000000 | bytes 2000000 | tf_op jit(solution)/shard_map/attend_backward/pallas_call | solution.py:208
  129.4 4.1 %attend_backward.7 = (bf16[512,384]{1,0:T(8,128)(2,1)S(1)}, bf16[8,64,384]{2,1,0:T(8,128)(2,1)S(1)}, f32[2,128]{1,0:T(2,128)S(1)}) custom-call(s32[1]{0:T(128)} %bitcast.3.place_ref, f32[2]{0:T(128)S(1)} %slice.283.alpha_ref, bf16[512,512]{1,0:T(8,128)(2,1)S(1)} %fusion.32.normed_ref, bf16[512,384]{1,0:T(8,128)(2,1)S(1)} %copy-done.12, ...), custom_call_target="tpu_custom_call" | custom-call | flops 3000000000 | bytes 2000000 | tf_op jit(solution)/shard_map/attend_backward/pallas_call | solution.py:208
  135.9 4.3 %attend_backward.6 = (bf16[512,384]{1,0:T(8,128)(2,1)S(1)}, bf16[8,64,384]{2,1,0:T(8,128)(2,1)S(1)}, f32[2,128]{1,0:T(2,128)S(1)}) custom-call(s32[1]{0:T(128)} %bitcast.3.place_ref, f32[2]{0:T(128)S(1)} %slice.282.alpha_ref, bf16[512,512]{1,0:T(8,128)(2,1)S(1)} %fusion.32.normed_ref, bf16[512,384]{1,0:T(8,128)(2,1)S(1)} %copy-done.10, ...), custom_call_target="tpu_custom_call" | custom-call | flops 3000000000 | bytes 2000000 | tf_op jit(solution)/shard_map/attend_backward/pallas_call | solution.py:208
  140.2 4.1 %attend_backward.5 = (bf16[512,384]{1,0:T(8,128)(2,1)S(1)}, bf16[8,64,384]{2,1,0:T(8,128)(2,1)S(1)}, f32[2,128]{1,0:T(2,128)S(1)}) custom-call(s32[1]{0:T(128)} %bitcast.3.place_ref, f32[2]{0:T(128)S(1)} %slice.281.alpha_ref, bf16[512,512]{1,0:T(8,128)(2,1)S(1)} %fusion.32.normed_ref, bf16[512,384]{1,0:T(8,128)(2,1)S(1)} %copy-done.8, ...), custom_call_target="tpu_custom_call" | custom-call | flops 3000000000 | bytes 2000000 | tf_op jit(solution)/shard_map/attend_backward/pallas_call | solution.py:208
  149.3 2.6 collective-permute-start.29
  155.3 4.8 %fusion.28 = bf16[512,512]{1,0:T(8,128)(2,1)S(1)} fusion(f32[512,512]{1,0:T(8,128)} %copy-done.19, bf16[2048,512]{1,0:T(8,128)(2,1)} %copy-done.59, f32[512]{0:T(512)S(1)} %copy-done.63, f32[512,2048]{1,0:T(8,128)} %copy-done.64, f32[2048]{0:T(1024)S(1)} %concatenate.138), kind=kOutput, calls=%fused_computation.71 | convolution fusion | flops 1085014016 | bytes 7874560 | tf_op jit(solution)/shard_map/dot_general | solution.py:37
  173.1 20.1 %collective-permute-done.46 = f32[514]{0:T(1024)S(1)} collective-permute-done((f32[514]{0:T(1024)S(1)}, f32[514]{0:T(1024)S(1)}, u32[]{:S(2)}, u32[]{:S(2)}) %collective-permute-start.46) | collective-permute-done | bytes 2088 | tf_op jit(solution)/shard_map/ppermute | solution.py:237
  194.7 18.9 %collective-permute-done.45 = f32[514]{0:T(1024)S(1)} collective-permute-done((f32[514]{0:T(1024)S(1)}, f32[514]{0:T(1024)S(1)}, u32[]{:S(2)}, u32[]{:S(2)}) %collective-permute-start.45) | collective-permute-done | bytes 2088 | tf_op jit(solution)/shard_map/ppermute | solution.py:237
  226.8 3.9 %collective-permute-done.53 = bf16[16,512]{1,0:T(8,128)(2,1)S(1)} collective-permute-done((bf16[16,512]{1,0:T(8,128)(2,1)S(1)}, bf16[16,512]{1,0:T(8,128)(2,1)S(1)}, u32[]{:S(2)}, u32[]{:S(2)}) %collective-permute-start.53) | collective-permute-done | bytes 16416 | tf_op jit(solution)/shard_map/ppermute | solution.py:237
  244.2 15.3 %collective-permute-done.20 = bf16[512,512]{1,0:T(8,128)(2,1)S(1)} collective-permute-done((bf16[512,512]{1,0:T(8,128)(2,1)S(1)}, bf16[512,512]{1,0:T(8,128)(2,1)S(1)}, u32[]{:S(2)}, u32[]{:S(2)}) %collective-permute-start.20) | collective-permute-done | bytes 524320 | tf_op jit(solution)/shard_map/ppermute | solution.py:237
  259.6 11.1 %select_bitcast_fusion.1 = (bf16[1,1024,512]{2,1,0:T(8,128)(2,1)S(1)}, bf16[1024,512]{1,0:T(8,128)(2,1)S(1)}, bf16[1024,512]{1,0:T(8,128)(2,1)S(1)}) fusion(pred[]{:T(512)S(6)} %eq.107, s32[]{:T(128)S(6)} %select_n.693, bf16[512,512]{1,0:T(8,128)(2,1)S(1)} %collective-permute-done.20, bf16[512,512]{1,0:T(8,128)(2,1)S(1)} %add_convert_fusion.2, ...), kind=kLoop, calls=%fused_computation.100 | loop fusion | flops 8912896 | bytes 5242889 | tf_op jit(solution)/shard_map/stack | solution.py:371
  270.8 8.7 %collective-permute-done.18 = bf16[512,512]{1,0:T(8,128)(2,1)S(1)} collective-permute-done((bf16[512,512]{1,0:T(8,128)(2,1)S(1)}, bf16[512,512]{1,0:T(8,128)(2,1)S(1)}, u32[]{:S(2)}, u32[]{:S(2)}) %collective-permute-start.18) | collective-permute-done | bytes 524320 | tf_op jit(solution)/shard_map/ppermute | solution.py:237
  279.6 11.2 %select_bitcast_fusion.3 = (bf16[1,1024,512]{2,1,0:T(8,128)(2,1)S(1)}, bf16[1024,512]{1,0:T(8,128)(2,1)S(1)}, bf16[1024,512]{1,0:T(8,128)(2,1)S(1)}) fusion(pred[]{:T(512)S(6)} %eq.107, s32[]{:T(128)S(6)} %select_n.693, bf16[512,512]{1,0:T(8,128)(2,1)S(1)} %collective-permute-done.17, bf16[512,512]{1,0:T(8,128)(2,1)S(1)} %fusion.28, s32[]{:T(128)S(6)} %select_n.695, ...), kind=kLoop, calls=%fused_computation.105 | loop fusion | flops 8912896 | bytes 5242889 | tf_op jit(solution)/shard_map/stack | solution.py:371
  296.8 3.2 collective-permute-done.36
  324.6 11.1 %collective-permute-done.59 = bf16[4,128,512]{2,1,0:T(8,128)(2,1)S(1)} collective-permute-done((bf16[4,128,512]{2,1,0:T(8,128)(2,1)S(1)}, bf16[4,128,512]{2,1,0:T(8,128)(2,1)S(1)}, u32[]{:S(2)}, u32[]{:S(2)}) %collective-permute-start.59) | collective-permute-done | bytes 524320 | tf_op jit(solution)/shard_map/ppermute | solution.py:234
  335.7 10.5 %collective-permute-done.61 = bf16[4,128,512]{2,1,0:T(8,128)(2,1)S(1)} collective-permute-done((bf16[4,128,512]{2,1,0:T(8,128)(2,1)S(1)}, bf16[4,128,512]{2,1,0:T(8,128)(2,1)S(1)}, u32[]{:S(2)}, u32[]{:S(2)}) %collective-permute-start.61) | collective-permute-done | bytes 524320 | tf_op jit(solution)/shard_map/ppermute | solution.py:234
  351.6 3.0 collective-permute-done.62
  356.7 4.2 %collective-permute-done.63 = bf16[128,512]{1,0:T(8,128)(2,1)S(1)} collective-permute-done((bf16[128,512]{1,0:T(8,128)(2,1)S(1)}, bf16[128,512]{1,0:T(8,128)(2,1)S(1)}, u32[]{:S(2)}, u32[]{:S(2)}) %collective-permute-start.63) | collective-permute-done | bytes 131104 | tf_op jit(solution)/shard_map/ppermute | solution.py:237
  (527 shorter events, 154.8 us)
Async XLA Ops:
  2.1 40.1 %collective-permute-start.9 = (f32[514]{0:T(1024)S(1)}, f32[514]{0:T(1024)S(1)}, u32[]{:S(2)}, u32[]{:S(2)}) collective-permute-start(f32[514]{0:T(1024)S(1)} %constant_dynamic-update-slice_fusion.134), channel_id=1, source_target_pairs={{0,3},{1,2},{2,1},{3,0},{4,7},{5,6},{6,5},{7,4},{8,11},{9,10},{10,... | collective-permute-start | bytes 6176 | tf_op jit(solution)/shard_map/ppermute | solution.py:237
  7.1 35.9 %collective-permute-start.8 = (f32[514]{0:T(1024)S(1)}, f32[514]{0:T(1024)S(1)}, u32[]{:S(2)}, u32[]{:S(2)}) collective-permute-start(f32[514]{0:T(1024)S(1)} %constant_dynamic-update-slice_fusion.134), channel_id=1, source_target_pairs={{0,2},{1,3},{2,0},{3,1},{4,6},{5,7},{6,4},{7,5},{8,10},{9,11},{10,... | collective-permute-start | bytes 6176 | tf_op jit(solution)/shard_map/ppermute | solution.py:237
  7.1 39.7 %collective-permute-start = (f32[514]{0:T(1024)S(1)}, f32[514]{0:T(1024)S(1)}, u32[]{:S(2)}, u32[]{:S(2)}) collective-permute-start(f32[514]{0:T(1024)S(1)} %constant_dynamic-update-slice_fusion.134), channel_id=1, source_target_pairs={{0,1},{1,0},{2,3},{3,2},{4,5},{5,4},{6,7},{7,6},{8,9},{9,8},{10,11... | collective-permute-start | bytes 6176 | tf_op jit(solution)/shard_map/ppermute | solution.py:237
  9.1 38.0 %collective-permute-start.3 = (bf16[64,384]{1,0:T(8,128)(2,1)S(1)}, bf16[64,384]{1,0:T(8,128)(2,1)S(1)}, u32[]{:S(2)}, u32[]{:S(2)}) collective-permute-start(bf16[64,384]{1,0:T(8,128)(2,1)S(1)} %constant_dynamic-slice_fusion.147), channel_id=1, source_target_pairs={{0,3},{1,2},{2,1},{3,0},{4,7},{5,6},{6,5},{7,4},{8,11},{9,10},{10,... | collective-permute-start | bytes 147464 | tf_op jit(solution)/shard_map/ppermute | solution.py:237
  13.0 34.8 %collective-permute-start.2 = (bf16[64,384]{1,0:T(8,128)(2,1)S(1)}, bf16[64,384]{1,0:T(8,128)(2,1)S(1)}, u32[]{:S(2)}, u32[]{:S(2)}) collective-permute-start(bf16[64,384]{1,0:T(8,128)(2,1)S(1)} %constant_dynamic-slice_fusion.147), channel_id=1, source_target_pairs={{0,2},{1,3},{2,0},{3,1},{4,6},{5,7},{6,4},{7,5},{8,10},{9,11},{10,... | collective-permute-start | bytes 147464 | tf_op jit(solution)/shard_map/ppermute | solution.py:237
  48.0 12.7 %collective-permute-start.5 = (bf16[3,64,384]{2,1,0:T(8,128)(2,1)S(1)}, bf16[3,64,384]{2,1,0:T(8,128)(2,1)S(1)}, u32[]{:S(2)}, u32[]{:S(2)}) collective-permute-start(bf16[3,64,384]{2,1,0:T(8,128)(2,1)S(1)} %get-tuple-element.211), channel_id=1, source_target_pairs={{0,16},{4,20},{8,24},{12,28},{16,0},{20,4},{24,8},{28,12},{1,17},{... | collective-permute-start | bytes 442376 | tf_op jit(solution)/shard_map/ppermute | solution.py:234
  49.6 11.7 %collective-permute-start.4 = (bf16[3,64,384]{2,1,0:T(8,128)(2,1)S(1)}, bf16[3,64,384]{2,1,0:T(8,128)(2,1)S(1)}, u32[]{:S(2)}, u32[]{:S(2)}) collective-permute-start(bf16[3,64,384]{2,1,0:T(8,128)(2,1)S(1)} %get-tuple-element.211), channel_id=1, source_target_pairs={{0,8},{4,12},{8,0},{12,4},{16,24},{20,28},{24,16},{28,20},{1,9},{5... | collective-permute-start | bytes 442376 | tf_op jit(solution)/shard_map/ppermute | solution.py:234
  57.6 12.3 %collective-permute-start.14 = (bf16[3,144,512]{2,1,0:T(8,128)(2,1)S(1)}, bf16[3,144,512]{2,1,0:T(8,128)(2,1)S(1)}, u32[]{:S(2)}, u32[]{:S(2)}) collective-permute-start(bf16[3,144,512]{2,1,0:T(8,128)(2,1)S(1)} %get-tuple-element.195), channel_id=1, source_target_pairs={{0,16},{4,20},{8,24},{12,28},{16,0},{20,4},{24,8},{28,12},{1,17},{... | collective-permute-start | bytes 1327112 | tf_op jit(solution)/shard_map/ppermute | solution.py:234
  59.2 13.1 %collective-permute-start.13 = (bf16[3,144,512]{2,1,0:T(8,128)(2,1)S(1)}, bf16[3,144,512]{2,1,0:T(8,128)(2,1)S(1)}, u32[]{:S(2)}, u32[]{:S(2)}) collective-permute-start(bf16[3,144,512]{2,1,0:T(8,128)(2,1)S(1)} %get-tuple-element.195), channel_id=1, source_target_pairs={{0,8},{4,12},{8,0},{12,4},{16,24},{20,28},{24,16},{28,20},{1,9},{5... | collective-permute-start | bytes 1327112 | tf_op jit(solution)/shard_map/ppermute | solution.py:234
  60.7 18.3 %collective-permute-start.15 = (bf16[3,144,512]{2,1,0:T(8,128)(2,1)S(1)}, bf16[3,144,512]{2,1,0:T(8,128)(2,1)S(1)}, u32[]{:S(2)}, u32[]{:S(2)}) collective-permute-start(bf16[3,144,512]{2,1,0:T(8,128)(2,1)S(1)} %get-tuple-element.195), channel_id=1, source_target_pairs={{0,24},{4,28},{8,16},{12,20},{16,8},{20,12},{24,0},{28,4},{1,25},{... | collective-permute-start | bytes 1327112 | tf_op jit(solution)/shard_map/ppermute | solution.py:234
  61.3 18.1 %collective-permute-start.7 = (bf16[4,3,64,384]{3,2,1,0:T(8,128)(2,1)S(1)}, bf16[4,3,64,384]{3,2,1,0:T(8,128)(2,1)S(1)}, u32[]{:S(2)}, u32[]{:S(2)}) collective-permute-start(bf16[4,3,64,384]{3,2,1,0:T(8,128)(2,1)S(1)} %pad_maximum_fusion.5), channel_id=1, source_target_pairs={{0,4},{4,0},{8,12},{12,8},{16,20},{20,16},{24,28},{28,24},{1,5},{5... | collective-permute-start | bytes 1769480 | tf_op jit(solution)/shard_map/ppermute | solution.py:234
  79.2 20.4 %collective-permute-start.16 = (bf16[4,3,144,512]{3,2,1,0:T(8,128)(2,1)S(1)}, bf16[4,3,144,512]{3,2,1,0:T(8,128)(2,1)S(1)}, u32[]{:S(2)}, u32[]{:S(2)}) collective-permute-start(bf16[4,3,144,512]{3,2,1,0:T(8,128)(2,1)S(1)} %pad_maximum_fusion.3), channel_id=1, source_target_pairs={{0,4},{4,0},{8,12},{12,8},{16,20},{20,16},{24,28},{28,24},{1,5},{5... | collective-permute-start | bytes 5308424 | tf_op jit(solution)/shard_map/ppermute | solution.py:234
  149.3 15.4 %collective-permute-start.29 = (f32[4616]{0:T(1024)S(1)}, f32[4616]{0:T(1024)S(1)}, u32[]{:S(2)}, u32[]{:S(2)}) collective-permute-start(f32[4616]{0:T(1024)S(1)} %constant_dynamic-update-slice_fusion.138), channel_id=1, source_target_pairs={{0,28},{4,24},{8,20},{12,16},{16,12},{20,8},{24,4},{28,0},{1,29},{... | collective-permute-start | bytes 55400 | tf_op jit(solution)/shard_map/ppermute | solution.py:234
  151.8 13.4 %collective-permute-start.28 = (f32[4616]{0:T(1024)S(1)}, f32[4616]{0:T(1024)S(1)}, u32[]{:S(2)}, u32[]{:S(2)}) collective-permute-start(f32[4616]{0:T(1024)S(1)} %constant_dynamic-update-slice_fusion.138), channel_id=1, source_target_pairs={{0,24},{4,28},{8,16},{12,20},{16,8},{20,12},{24,0},{28,4},{1,25},{... | collective-permute-start | bytes 55400 | tf_op jit(solution)/shard_map/ppermute | solution.py:234
  152.3 13.2 %collective-permute-start.27 = (f32[4616]{0:T(1024)S(1)}, f32[4616]{0:T(1024)S(1)}, u32[]{:S(2)}, u32[]{:S(2)}) collective-permute-start(f32[4616]{0:T(1024)S(1)} %constant_dynamic-update-slice_fusion.138), channel_id=1, source_target_pairs={{0,20},{4,16},{8,28},{12,24},{16,4},{20,0},{24,12},{28,8},{1,21},{... | collective-permute-start | bytes 55400 | tf_op jit(solution)/shard_map/ppermute | solution.py:234
  153.2 13.7 %collective-permute-start.26 = (f32[4616]{0:T(1024)S(1)}, f32[4616]{0:T(1024)S(1)}, u32[]{:S(2)}, u32[]{:S(2)}) collective-permute-start(f32[4616]{0:T(1024)S(1)} %constant_dynamic-update-slice_fusion.138), channel_id=1, source_target_pairs={{0,16},{4,20},{8,24},{12,28},{16,0},{20,4},{24,8},{28,12},{1,17},{... | collective-permute-start | bytes 55400 | tf_op jit(solution)/shard_map/ppermute | solution.py:234
  153.9 13.4 %collective-permute-start.25 = (f32[4616]{0:T(1024)S(1)}, f32[4616]{0:T(1024)S(1)}, u32[]{:S(2)}, u32[]{:S(2)}) collective-permute-start(f32[4616]{0:T(1024)S(1)} %constant_dynamic-update-slice_fusion.138), channel_id=1, source_target_pairs={{0,12},{4,8},{8,4},{12,0},{16,28},{20,24},{24,20},{28,16},{1,13},{... | collective-permute-start | bytes 55400 | tf_op jit(solution)/shard_map/ppermute | solution.py:234
  165.5 76.6 %collective-permute-start.22 = (bf16[512,512]{1,0:T(8,128)(2,1)S(1)}, bf16[512,512]{1,0:T(8,128)(2,1)S(1)}, u32[]{:S(2)}, u32[]{:S(2)}) collective-permute-start(bf16[512,512]{1,0:T(8,128)(2,1)S(1)} %add_convert_fusion.2), channel_id=1, source_target_pairs={{0,3},{1,2},{2,1},{3,0},{4,7},{5,6},{6,5},{7,4},{8,11},{9,10},{10,... | collective-permute-start | bytes 1572872 | tf_op jit(solution)/shard_map/ppermute | solution.py:237
  166.9 77.3 %collective-permute-start.21 = (bf16[512,512]{1,0:T(8,128)(2,1)S(1)}, bf16[512,512]{1,0:T(8,128)(2,1)S(1)}, u32[]{:S(2)}, u32[]{:S(2)}) collective-permute-start(bf16[512,512]{1,0:T(8,128)(2,1)S(1)} %add_convert_fusion.2), channel_id=1, source_target_pairs={{0,2},{1,3},{2,0},{3,1},{4,6},{5,7},{6,4},{7,5},{8,10},{9,11},{10,... | collective-permute-start | bytes 1572872 | tf_op jit(solution)/shard_map/ppermute | solution.py:237
  168.6 24.6 %collective-permute-start.46 = (f32[514]{0:T(1024)S(1)}, f32[514]{0:T(1024)S(1)}, u32[]{:S(2)}, u32[]{:S(2)}) collective-permute-start(f32[514]{0:T(1024)S(1)} %get-tuple-element.215), channel_id=1, source_target_pairs={{0,3},{1,2},{2,1},{3,0},{4,7},{5,6},{6,5},{7,4},{8,11},{9,10},{10,... | collective-permute-start | bytes 6176 | tf_op jit(solution)/shard_map/ppermute | solution.py:237
  170.0 43.6 %collective-permute-start.45 = (f32[514]{0:T(1024)S(1)}, f32[514]{0:T(1024)S(1)}, u32[]{:S(2)}, u32[]{:S(2)}) collective-permute-start(f32[514]{0:T(1024)S(1)} %get-tuple-element.216), channel_id=1, source_target_pairs={{0,2},{1,3},{2,0},{3,1},{4,6},{5,7},{6,4},{7,5},{8,10},{9,11},{10,... | collective-permute-start | bytes 6176 | tf_op jit(solution)/shard_map/ppermute | solution.py:237
  171.6 44.6 %collective-permute-start.44 = (f32[514]{0:T(1024)S(1)}, f32[514]{0:T(1024)S(1)}, u32[]{:S(2)}, u32[]{:S(2)}) collective-permute-start(f32[514]{0:T(1024)S(1)} %get-tuple-element.217), channel_id=1, source_target_pairs={{0,1},{1,0},{2,3},{3,2},{4,5},{5,4},{6,7},{7,6},{8,9},{9,8},{10,11... | collective-permute-start | bytes 6176 | tf_op jit(solution)/shard_map/ppermute | solution.py:237
  193.2 24.5 %collective-permute-start.48 = (bf16[4,16,512]{2,1,0:T(8,128)(2,1)S(1)}, bf16[4,16,512]{2,1,0:T(8,128)(2,1)S(1)}, u32[]{:S(2)}, u32[]{:S(2)}) collective-permute-start(bf16[4,16,512]{2,1,0:T(8,128)(2,1)S(1)} %get-tuple-element.204), channel_id=1, source_target_pairs={{0,8},{4,12},{8,0},{12,4},{16,24},{20,28},{24,16},{28,20},{1,9},{5... | collective-permute-start | bytes 196616 | tf_op jit(solution)/shard_map/ppermute | solution.py:234
  236.1 23.4 %collective-permute-start.20 = (bf16[512,512]{1,0:T(8,128)(2,1)S(1)}, bf16[512,512]{1,0:T(8,128)(2,1)S(1)}, u32[]{:S(2)}, u32[]{:S(2)}) collective-permute-start(bf16[512,512]{1,0:T(8,128)(2,1)S(1)} %add_convert_fusion.2), channel_id=1, source_target_pairs={{0,1},{1,0},{2,3},{3,2},{4,5},{5,4},{6,7},{7,6},{8,9},{9,8},{10,11... | collective-permute-start | bytes 1572872 | tf_op jit(solution)/shard_map/ppermute | solution.py:237
  237.6 33.2 %collective-permute-start.19 = (bf16[512,512]{1,0:T(8,128)(2,1)S(1)}, bf16[512,512]{1,0:T(8,128)(2,1)S(1)}, u32[]{:S(2)}, u32[]{:S(2)}) collective-permute-start(bf16[512,512]{1,0:T(8,128)(2,1)S(1)} %fusion.28), channel_id=1, source_target_pairs={{0,3},{1,2},{2,1},{3,0},{4,7},{5,6},{6,5},{7,4},{8,11},{9,10},{10,... | collective-permute-start | bytes 1572872 | tf_op jit(solution)/shard_map/ppermute | solution.py:237
  241.2 38.4 %collective-permute-start.18 = (bf16[512,512]{1,0:T(8,128)(2,1)S(1)}, bf16[512,512]{1,0:T(8,128)(2,1)S(1)}, u32[]{:S(2)}, u32[]{:S(2)}) collective-permute-start(bf16[512,512]{1,0:T(8,128)(2,1)S(1)} %fusion.28), channel_id=1, source_target_pairs={{0,2},{1,3},{2,0},{3,1},{4,6},{5,7},{6,4},{7,5},{8,10},{9,11},{10,... | collective-permute-start | bytes 1572872 | tf_op jit(solution)/shard_map/ppermute | solution.py:237
  242.1 37.5 %collective-permute-start.17 = (bf16[512,512]{1,0:T(8,128)(2,1)S(1)}, bf16[512,512]{1,0:T(8,128)(2,1)S(1)}, u32[]{:S(2)}, u32[]{:S(2)}) collective-permute-start(bf16[512,512]{1,0:T(8,128)(2,1)S(1)} %fusion.28), channel_id=1, source_target_pairs={{0,1},{1,0},{2,3},{3,2},{4,5},{5,4},{6,7},{7,6},{8,9},{9,8},{10,11... | collective-permute-start | bytes 1572872 | tf_op jit(solution)/shard_map/ppermute | solution.py:237
  244.2 46.5 %collective-permute-start.33 = (bf16[4,4,64,384]{3,2,1,0:T(8,128)(2,1)S(1)}, bf16[4,4,64,384]{3,2,1,0:T(8,128)(2,1)S(1)}, u32[]{:S(2)}, u32[]{:S(2)}) collective-permute-start(bf16[4,4,64,384]{3,2,1,0:T(8,128)(2,1)S(1)} %slice.392), channel_id=1, source_target_pairs={{0,4},{4,0},{8,12},{12,8},{16,20},{20,16},{24,28},{28,24},{1,5},{5... | collective-permute-start | bytes 2359304 | tf_op jit(solution)/shard_map/ppermute | solution.py:234
  259.5 58.7 %collective-permute-start.58 = (bf16[4,4,128,512]{3,2,1,0:T(8,128)(2,1)}, bf16[4,4,128,512]{3,2,1,0:T(8,128)(2,1)}, u32[]{:S(2)}, u32[]{:S(2)}) collective-permute-start(bf16[4,4,128,512]{3,2,1,0:T(8,128)(2,1)} %pad_maximum_fusion), channel_id=1, source_target_pairs={{0,4},{4,0},{8,12},{12,8},{16,20},{20,16},{24,28},{28,24},{1,5},{5... | collective-permute-start | bytes 6291464 | tf_op jit(solution)/shard_map/ppermute | solution.py:234
  320.9 14.8 %collective-permute-start.59 = (bf16[4,128,512]{2,1,0:T(8,128)(2,1)S(1)}, bf16[4,128,512]{2,1,0:T(8,128)(2,1)S(1)}, u32[]{:S(2)}, u32[]{:S(2)}) collective-permute-start(bf16[4,128,512]{2,1,0:T(8,128)(2,1)S(1)} %get-tuple-element.167), channel_id=1, source_target_pairs={{0,8},{4,12},{8,0},{12,4},{16,24},{20,28},{24,16},{28,20},{1,9},{5... | collective-permute-start | bytes 1572872 | tf_op jit(solution)/shard_map/ppermute | solution.py:234
  321.5 24.7 %collective-permute-start.61 = (bf16[4,128,512]{2,1,0:T(8,128)(2,1)S(1)}, bf16[4,128,512]{2,1,0:T(8,128)(2,1)S(1)}, u32[]{:S(2)}, u32[]{:S(2)}) collective-permute-start(bf16[4,128,512]{2,1,0:T(8,128)(2,1)S(1)} %get-tuple-element.168), channel_id=1, source_target_pairs={{0,24},{4,28},{8,16},{12,20},{16,8},{20,12},{24,0},{28,4},{1,25},{... | collective-permute-start | bytes 1572872 | tf_op jit(solution)/shard_map/ppermute | solution.py:234
  322.9 24.6 %collective-permute-start.60 = (bf16[4,128,512]{2,1,0:T(8,128)(2,1)S(1)}, bf16[4,128,512]{2,1,0:T(8,128)(2,1)S(1)}, u32[]{:S(2)}, u32[]{:S(2)}) collective-permute-start(bf16[4,128,512]{2,1,0:T(8,128)(2,1)S(1)} %get-tuple-element.169), channel_id=1, source_target_pairs={{0,16},{4,20},{8,24},{12,28},{16,0},{20,4},{24,8},{28,12},{1,17},{... | collective-permute-start | bytes 1572872 | tf_op jit(solution)/shard_map/ppermute | solution.py:234
  (102 other events, 462.8 us)
